TPU v7x, 32 devices: a whole 2x2x4 slice. The times are simulated.
32 devices in a mesh: fsdp: 4 (over y, core), ctx: 4 (over z), tp: 2 (over x).
Axes of the slice: x: 2, y: 2, z: 4, core: 2. Of those that a mesh axis runs over, the one named last changes fastest.
Arguments:
- tokens: bfloat16 [8, 2048, 960], P('fsdp', ('ctx', 'tp')), may hold values from -6 to 6
- cotangent: bfloat16 [8, 2048, 960], P('fsdp', ('ctx', 'tp')), may hold values from -6 to 6
- input_gain: bfloat16 [960], P('fsdp'), may hold values from 0.099609375 to 1.8984375
- w_query: bfloat16 [960, 960], P('fsdp'), may hold values from -0.1875 to 0.1875
- w_keyval: bfloat16 [960, 640], P('fsdp'), may hold values from -0.1875 to 0.1875
- w_output: bfloat16 [960, 960], P('fsdp'), may hold values from -2 to 2
- middle_gain: bfloat16 [960], P('fsdp'), may hold values from 0.099609375 to 1.8984375
- w_gate: bfloat16 [960, 2560], P('fsdp', 'tp'), may hold values from -0.1875 to 0.1875
- w_up: bfloat16 [960, 2560], P('fsdp', 'tp'), may hold values from -0.1875 to 0.1875
- w_down: bfloat16 [960, 2560], P('fsdp', 'tp'), may hold values from -0.25 to 0.25
Outputs:
- result: bfloat16 [8, 2048, 960], P('fsdp', ('ctx', 'tp'))
- grad_tokens: float32 [8, 2048, 960], P('fsdp', ('ctx', 'tp'))
- grad_input_gain: float32 [960], P('fsdp')
- grad_w_query: float32 [960, 960], P('fsdp')
- grad_w_keyval: float32 [960, 640], P('fsdp')
- grad_w_output: float32 [960, 960], P('fsdp')
- grad_middle_gain: float32 [960], P('fsdp')
- grad_w_gate: float32 [960, 2560], P('fsdp', 'tp')
- grad_w_up: float32 [960, 2560], P('fsdp', 'tp')
- grad_w_down: float32 [960, 2560], P('fsdp', 'tp')
All inputs are finite; a program needn't handle non-finite values.
Results may differ from a plain program's by a relative error of at most 0.02.
Values may be sent and summed in bfloat16 or wider, within the bound.
A program may use at most 128 MiB of HBM per device.

v0:
```python
from functools import partial
import jax
import jax.numpy as jnp
from jax import lax
from jax.sharding import PartitionSpec as P

QUERY_HEADS = 15
KEYVAL_HEADS = 5
HEAD_WIDTH = 64
SEQUENCE_LENGTH = 2048
KEY_WIDTH = 320
EPS = 1e-05
THETA = 10000.0


def rope_tables(token_positions, first_place):
    half_width = HEAD_WIDTH // 2
    position = (first_place + lax.iota(jnp.int32, token_positions)).astype(jnp.float32)
    frequency = THETA ** (-(2.0 * lax.iota(jnp.int32, half_width).astype(jnp.float32)) / HEAD_WIDTH)
    angles = position[:, None] * frequency[None, :]
    return (jnp.cos(angles), jnp.sin(angles))


def apply_rotary(value_rows, cosine_table, sine_table, heads):
    half_width = HEAD_WIDTH // 2
    shaped = value_rows.reshape(value_rows.shape[:-1] + (heads, HEAD_WIDTH))
    leading = shaped[..., :half_width]
    trailing = shaped[..., half_width:]
    cosine_wide = cosine_table[:, None, :]
    sine_wide = sine_table[:, None, :]
    turned = jnp.concatenate(
        [
            leading * cosine_wide - trailing * sine_wide,
            trailing * cosine_wide + leading * sine_wide,
        ],
        -1,
    )
    return turned.reshape(value_rows.shape)


def normalize(value_rows):
    inverse_rms = lax.rsqrt(jnp.mean(value_rows * value_rows, -1, keepdims=True) + EPS)
    return (value_rows * inverse_rms, inverse_rms)


def norm_back(back_unit, unit_rows, inverse_rms):
    return inverse_rms * (
        back_unit - unit_rows * jnp.mean(back_unit * unit_rows, -1, keepdims=True)
    )


def to_heads(value_rows, sequence_count, token_positions):
    group_total = QUERY_HEADS // KEYVAL_HEADS
    return (
        value_rows.reshape(sequence_count, token_positions, KEYVAL_HEADS, group_total, HEAD_WIDTH)
        .transpose(0, 2, 3, 1, 4)
        .reshape(sequence_count * KEYVAL_HEADS, group_total * token_positions, HEAD_WIDTH)
    )


def from_heads(value_rows, sequence_count, token_positions):
    group_total = QUERY_HEADS // KEYVAL_HEADS
    return (
        value_rows.reshape(sequence_count, KEYVAL_HEADS, group_total, token_positions, HEAD_WIDTH)
        .transpose(0, 3, 1, 2, 4)
        .reshape(sequence_count, token_positions, QUERY_HEADS * HEAD_WIDTH)
    )


def per_sequence(value_rows, sequence_count):
    return value_rows.reshape((sequence_count, KEYVAL_HEADS) + value_rows.shape[1:])


def masked_scores(query_group, key_group, allowed):
    raw_scores = jnp.einsum("qd,kd->qk", query_group, key_group, preferred_element_type=jnp.float32)
    return jnp.where(allowed, raw_scores * HEAD_WIDTH ** (-0.5), -jnp.inf)


def head_forward(head_items, allowed):
    query_group, key_group, value_group = head_items
    scores = masked_scores(query_group, key_group, allowed)
    row_top = jnp.max(scores, -1, keepdims=True)
    lifted = jnp.exp(scores - row_top)
    row_total = jnp.sum(lifted, -1, keepdims=True)
    weights = (lifted / row_total).astype(jnp.bfloat16)
    mixed_heads = jnp.einsum("qk,kd->qd", weights, value_group, preferred_element_type=jnp.float32)
    return (mixed_heads, row_top[:, 0], row_total[:, 0])


def head_backward(head_items, allowed):
    query_group, key_group, value_group, back_mixed, row_top, row_total = head_items
    scores = masked_scores(query_group, key_group, allowed)
    weights = jnp.exp(scores - row_top[:, None]) / row_total[:, None]
    back_weights = jnp.einsum(
        "qd,kd->qk", back_mixed, value_group, preferred_element_type=jnp.float32
    )
    weighted_sum = jnp.sum(weights * back_weights, -1, keepdims=True)
    back_scores = (weights * (back_weights - weighted_sum)).astype(jnp.bfloat16)
    back_query = jnp.einsum(
        "qk,kd->qd", back_scores, key_group, preferred_element_type=jnp.float32
    ) * HEAD_WIDTH ** (-0.5)
    back_key = jnp.einsum(
        "qk,qd->kd", back_scores, query_group, preferred_element_type=jnp.float32
    ) * HEAD_WIDTH ** (-0.5)
    back_value = jnp.einsum(
        "qk,qd->kd", weights.astype(jnp.bfloat16), back_mixed, preferred_element_type=jnp.float32
    )
    return (back_query, back_key, back_value)


def on_device(
    tokens, cotangent, input_gain, w_query, w_keyval, w_output, middle_gain, w_gate, w_up, w_down
):
    sequence_count = tokens.shape[0]
    token_positions = tokens.shape[1]
    group_total = QUERY_HEADS // KEYVAL_HEADS
    place_index = lax.axis_index("ctx") * lax.axis_size("tp") + lax.axis_index("tp")
    first_place = place_index * token_positions
    cosine_table, sine_table = rope_tables(token_positions, first_place)
    query_place = first_place + lax.iota(jnp.int32, group_total * token_positions) % token_positions
    allowed = lax.iota(jnp.int32, SEQUENCE_LENGTH)[None, :] <= query_place[:, None]
    full_gain_one, full_query, full_keyval, full_output = (
        lax.all_gather(input_gain, "fsdp", axis=0, tiled=True),
        lax.all_gather(w_query, "fsdp", axis=0, tiled=True),
        lax.all_gather(w_keyval, "fsdp", axis=0, tiled=True),
        lax.all_gather(w_output, "fsdp", axis=0, tiled=True),
    )
    gain_one = full_gain_one.astype(jnp.float32)
    inputs = tokens.astype(jnp.float32)
    unit_one, inverse_one = normalize(inputs)
    normed_one = (unit_one * gain_one).astype(jnp.bfloat16)
    query_raw = jnp.dot(normed_one, full_query, preferred_element_type=jnp.float32)
    keyval_unrotated = jnp.dot(normed_one, full_keyval, preferred_element_type=jnp.float32)
    query_low = apply_rotary(query_raw, cosine_table, sine_table, QUERY_HEADS).astype(jnp.bfloat16)
    keyval_low = jnp.concatenate(
        [
            apply_rotary(keyval_unrotated[..., :KEY_WIDTH], cosine_table, sine_table, KEYVAL_HEADS),
            keyval_unrotated[..., KEY_WIDTH:],
        ],
        -1,
    ).astype(jnp.bfloat16)
    keyval_gathered = lax.all_gather(keyval_low, ("ctx", "tp"), axis=1, tiled=True)
    query_heads = to_heads(query_low, sequence_count, token_positions)
    stacked = (
        keyval_gathered.reshape(sequence_count, SEQUENCE_LENGTH, 2, KEYVAL_HEADS, HEAD_WIDTH)
        .transpose(2, 0, 3, 1, 4)
        .reshape(2, sequence_count * KEYVAL_HEADS, SEQUENCE_LENGTH, HEAD_WIDTH)
    )
    key_heads = stacked[0]
    value_heads = stacked[1]
    mixed_heads, row_top, row_total = lax.map(
        partial(head_forward, allowed=allowed), (query_heads, key_heads, value_heads)
    )
    mixed_low = from_heads(mixed_heads, sequence_count, token_positions).astype(jnp.bfloat16)
    attention_out = jnp.dot(mixed_low, full_output, preferred_element_type=jnp.float32)
    middle = inputs + attention_out
    full_gate, full_up, full_down, full_gain_two = (
        lax.all_gather(w_gate, "fsdp", axis=0, tiled=True),
        lax.all_gather(w_up, "fsdp", axis=0, tiled=True),
        lax.all_gather(w_down, "fsdp", axis=0, tiled=True),
        lax.all_gather(middle_gain, "fsdp", axis=0, tiled=True),
    )
    gain_two = full_gain_two.astype(jnp.float32)
    unit_two, inverse_two = normalize(middle)
    normed_two = (unit_two * gain_two).astype(jnp.bfloat16)
    pair_rows, pair_cotangent = (
        lax.all_gather(normed_two, "tp", axis=1, tiled=True),
        lax.all_gather(cotangent, "tp", axis=1, tiled=True),
    )
    gate_proj = jnp.dot(pair_rows, full_gate, preferred_element_type=jnp.float32)
    up_proj = jnp.dot(pair_rows, full_up, preferred_element_type=jnp.float32)
    sigmoid_gate = jax.nn.sigmoid(gate_proj)
    swish_gate = gate_proj * sigmoid_gate
    hidden = (swish_gate * up_proj).astype(jnp.bfloat16)
    branch_part = jnp.einsum("spf,df->spd", hidden, full_down, preferred_element_type=jnp.float32)
    feed_out = lax.psum_scatter(
        branch_part.astype(jnp.bfloat16), "tp", scatter_dimension=1, tiled=True
    ).astype(jnp.float32)
    result = (middle + feed_out).astype(jnp.bfloat16)
    back_hidden = jnp.dot(pair_cotangent, full_down, preferred_element_type=jnp.float32)
    back_gate = (
        back_hidden * up_proj * sigmoid_gate * (1.0 + gate_proj * (1.0 - sigmoid_gate))
    ).astype(jnp.bfloat16)
    back_up = (back_hidden * swish_gate).astype(jnp.bfloat16)
    grad_down = jnp.einsum(
        "spd,spf->df", pair_cotangent, hidden, preferred_element_type=jnp.float32
    )
    grad_gate = jnp.einsum("spd,spf->df", pair_rows, back_gate, preferred_element_type=jnp.float32)
    grad_up = jnp.einsum("spd,spf->df", pair_rows, back_up, preferred_element_type=jnp.float32)
    back_normed_part = jnp.einsum(
        "spf,df->spd", back_gate, full_gate, preferred_element_type=jnp.float32
    ) + jnp.einsum("spf,df->spd", back_up, full_up, preferred_element_type=jnp.float32)
    back_normed_two = lax.psum_scatter(back_normed_part, "tp", scatter_dimension=1, tiled=True)
    grad_gain_two = jnp.sum(back_normed_two * unit_two, axis=(0, 1))
    back_middle = cotangent.astype(jnp.float32) + norm_back(
        back_normed_two * gain_two, unit_two, inverse_two
    )
    back_attention = back_middle.astype(jnp.bfloat16)
    grad_output = jnp.einsum(
        "spq,spd->qd", mixed_low, back_attention, preferred_element_type=jnp.float32
    )
    back_mixed = jnp.einsum(
        "spd,qd->spq", back_attention, full_output, preferred_element_type=jnp.float32
    ).astype(jnp.bfloat16)

    def attend_back(carried, sequence_items):
        back_query, back_key, back_value = lax.map(
            partial(head_backward, allowed=allowed), sequence_items
        )
        back_keyval = (
            jnp.stack([back_key, back_value])
            .transpose(2, 0, 1, 3)
            .reshape(SEQUENCE_LENGTH, 2 * KEY_WIDTH)
        )
        owned_rows = lax.psum_scatter(
            back_keyval.astype(jnp.bfloat16), ("ctx", "tp"), scatter_dimension=0, tiled=True
        ).astype(jnp.float32)
        return (carried, (back_query, owned_rows))

    sequence_items = tuple(
        (
            per_sequence(value_rows, sequence_count)
            for value_rows in (
                query_heads,
                key_heads,
                value_heads,
                to_heads(back_mixed, sequence_count, token_positions),
                row_top,
                row_total,
            )
        )
    )
    unused, (query_gradient_full, owned_tokens_full) = lax.scan(
        attend_back, jnp.zeros((), jnp.float32), sequence_items
    )
    back_query_rows = from_heads(
        query_gradient_full.reshape(
            (sequence_count * KEYVAL_HEADS,) + query_gradient_full.shape[2:]
        ),
        sequence_count,
        token_positions,
    )
    back_query_low = apply_rotary(back_query_rows, cosine_table, -sine_table, QUERY_HEADS).astype(
        jnp.bfloat16
    )
    back_keyval_low = jnp.concatenate(
        [
            apply_rotary(
                owned_tokens_full[..., :KEY_WIDTH], cosine_table, -sine_table, KEYVAL_HEADS
            ),
            owned_tokens_full[..., KEY_WIDTH:],
        ],
        -1,
    ).astype(jnp.bfloat16)
    grad_query = jnp.einsum(
        "spd,spq->dq", normed_one, back_query_low, preferred_element_type=jnp.float32
    )
    grad_keyval = jnp.einsum(
        "spd,spk->dk", normed_one, back_keyval_low, preferred_element_type=jnp.float32
    )
    back_normed_one = jnp.einsum(
        "spq,dq->spd", back_query_low, full_query, preferred_element_type=jnp.float32
    ) + jnp.einsum("spk,dk->spd", back_keyval_low, full_keyval, preferred_element_type=jnp.float32)
    grad_gain_one = jnp.sum(back_normed_one * unit_one, axis=(0, 1))
    back_inputs = back_middle + norm_back(back_normed_one * gain_one, unit_one, inverse_one)
    attention_term = jnp.concatenate([grad_query, grad_keyval, grad_output], 1)
    feed_term = jnp.concatenate([grad_gate, grad_up, grad_down], 1)
    attention_total, gain_one_total, gain_two_total = (
        lax.psum(attention_term.astype(jnp.bfloat16), ("ctx", "tp")).astype(jnp.float32),
        lax.psum(grad_gain_one.astype(jnp.bfloat16), ("ctx", "tp")).astype(jnp.float32),
        lax.psum(grad_gain_two.astype(jnp.bfloat16), ("ctx", "tp")).astype(jnp.float32),
    )
    feed_total = lax.psum(feed_term.astype(jnp.bfloat16), "ctx")
    attention_share, feed_share, gain_one_share, gain_two_share = (
        lax.psum_scatter(
            attention_total.astype(jnp.bfloat16), "fsdp", scatter_dimension=0, tiled=True
        ).astype(jnp.float32),
        lax.psum_scatter(feed_total, "fsdp", scatter_dimension=0, tiled=True).astype(jnp.float32),
        lax.psum_scatter(
            gain_one_total.astype(jnp.bfloat16), "fsdp", scatter_dimension=0, tiled=True
        ).astype(jnp.float32),
        lax.psum_scatter(
            gain_two_total.astype(jnp.bfloat16), "fsdp", scatter_dimension=0, tiled=True
        ).astype(jnp.float32),
    )
    query_width = full_query.shape[1]
    keyval_width = full_keyval.shape[1]
    hidden_width = full_gate.shape[1]
    share_query = attention_share[:, :query_width]
    share_keyval = attention_share[:, query_width : query_width + keyval_width]
    share_output = attention_share[:, query_width + keyval_width :]
    share_gate = feed_share[:, :hidden_width]
    share_up = feed_share[:, hidden_width : 2 * hidden_width]
    share_down = feed_share[:, 2 * hidden_width :]
    return (
        result,
        back_inputs,
        gain_one_share,
        share_query,
        share_keyval,
        share_output,
        gain_two_share,
        share_gate,
        share_up,
        share_down,
    )


def solution(mesh):
    in_specs = (
        P("fsdp", ("ctx", "tp"), None),
        P("fsdp", ("ctx", "tp"), None),
        P("fsdp"),
        P("fsdp", None),
        P("fsdp", None),
        P("fsdp", None),
        P("fsdp"),
        P("fsdp", "tp"),
        P("fsdp", "tp"),
        P("fsdp", "tp"),
    )
    out_specs = (
        P("fsdp", ("ctx", "tp"), None),
        P("fsdp", ("ctx", "tp"), None),
        P("fsdp"),
        P("fsdp", None),
        P("fsdp", None),
        P("fsdp", None),
        P("fsdp"),
        P("fsdp", "tp"),
        P("fsdp", "tp"),
        P("fsdp", "tp"),
    )
    return jax.shard_map(
        on_device, mesh=mesh, in_specs=in_specs, out_specs=out_specs, check_vma=False
    )
```

profile of v0, /device:TPU:0, one launch (start us, length us, event | category | flops | bytes accessed | tf_op | source)
XLA Modules:
  0.0 1055.6 jit_solution(356635097389830232)
XLA Ops:
  12.4 8.3 all-reduce.6
  37.5 16.0 %all-gather.10.cloned.1.call-done = bf16[960,960]{1,0:T(8,128)(2,1)} async-done(((bf16[240,960]{1,0:T(8,128)(2,1)}), bf16[960,960]{1,0:T(8,128)(2,1)}) %all-gather.10.cloned.1.call-update) | async-done | bytes 1843216 | tf_op jit(solution)/shard_map/all_gather | solution.py:124
  58.6 84.0 %all-gather.14.cloned.1.call-done = bf16[2,2048,640]{2,1,0:T(8,128)(2,1)} async-done(((bf16[2,256,640]{2,1,0:T(8,128)(2,1)}), bf16[2,2048,640]{2,1,0:T(8,128)(2,1)}) %all-gather.14.cloned.1.call-update) | async-done | bytes 5242896 | tf_op jit(solution)/shard_map/all_gather | solution.py:142
  142.6 8.0 copy.72
  150.6 7.3 slice_bitcast_fusion
  157.9 80.6 %while.43 = (s32[]{:T(128)}, bf16[10,768,64]{1,2,0:T(8,128)(2,1)S(1)}, f32[10,768]{1,0:T(8,128)S(1)}, f32[10,768]{1,0:T(8,128)S(1)}, bf16[10,768,64]{2,1,0:T(8,1...) while((s32[]{:T(128)}, ...), condition=%wide.region_4.5_spmd.clone, body=%wide.region_1.4_spmd.clone.sunk | while | flops 426244608 | bytes 19846260 | solution.py:151
  248.7 7.6 fusion.58
  256.3 26.9 %all-gather.18.cloned.1.call-done = bf16[2,512,960]{1,2,0:T(8,128)(2,1)} async-done(((bf16[2,256,960]{1,2,0:T(8,128)(2,1)}), bf16[2,512,960]{1,2,0:T(8,128)(2,1)}) %all-gather.18.cloned.1.call-update) | async-done | bytes 1966096 | tf_op jit(solution)/shard_map/all_gather | solution.py:167
  283.1 7.6 fusion.64
  290.7 18.6 %all-gather.20.cloned.1.call-done = bf16[960,1280]{1,0:T(8,128)(2,1)} async-done(((bf16[240,1280]{1,0:T(8,128)(2,1)}), bf16[960,1280]{1,0:T(8,128)(2,1)}) %all-gather.20.cloned.1.call-update) | async-done | bytes 2457616 | tf_op jit(solution)/shard_map/all_gather | solution.py:158
  309.4 11.9 %multiply_convert_fusion.2 = (bf16[2,512,1280]{2,1,0:T(8,128)(2,1)S(1)}, bf16[2,512,1280]{2,1,0:T(8,128)(2,1)S(1)}, bf16[2,512,1280]{2,1,0:T(8,128)(2,1)}) fusion(f32[2,512,1280]{2,1,0:T(8,128)} %fusion.58, f32[2,512,1280]{2,1,0:T(8,128)} %fusion.64, bf16[2,512,960]{1,2,0:T(8,128)(2,1)} %all-gather.18.cloned.1.call-done, ...), kind=kOutput, calls=%fused_computation.71 | convolution fusion | flops 2536243200 | bytes 22773760 | tf_op jit(solution)/shard_map/dot_general | solution.py:170
  352.3 29.6 %reduce-scatter.8.cloned.1.call-done = f32[2,256,960]{1,2,0:T(8,128)} async-done(((f32[2,512,960]{1,2,0:T(8,128)}), f32[2,256,960]{1,2,0:T(8,128)}) %reduce-scatter.8.cloned.1.call-update) | async-done | bytes 1966096 | tf_op jit(solution)/shard_map/reduce_scatter | solution.py:193
  384.5 30.1 %reduce-scatter.6.cloned.1.call-done = bf16[2,256,960]{1,2,0:T(8,128)(2,1)} async-done(((bf16[2,512,960]{1,2,0:T(8,128)(2,1)}), bf16[2,256,960]{1,2,0:T(8,128)(2,1)}) %reduce-scatter.6.cloned.1.call-update) | async-done | bytes 983056 | tf_op jit(solution)/shard_map/reduce_scatter | solution.py:176
  421.2 340.2 %while.45 = (s32[]{:T(128)}, f32[2,5,768,64]{2,3,1,0:T(8,128)}, f32[2,256,640]{1,2,0:T(8,128)}, bf16[2,5,768,64]{3,2,1,0:T(8,128)(2,1)}, bf16[2,5,2048,64]{2,3,1...) while((s32[]{:T(128)}, f32[2,5,768,64]{2,3,1,0:T(8,128)}, ...), condition=%wide.region_14.15_spmd.clone, body=%wide.region_9.14_spmd.clone.sunk | while | flops 1025588480 | bytes 125203080 | solution.py:233
  435.6 79.8 %while.46 = (s32[]{:T(128)}, f32[5,768,64]{1,2,0:T(8,128)}, bf16[5,2048,64]{1,2,0:T(8,128)(2,1)}, bf16[5,2048,64]{1,2,0:T(8,128)(2,1)}, bf16[5,768,64]{2,1,0:T(8...) while((s32[]{:T(128)}, f32[5,768,64]{1,2,0:T(8,128)}, ...), condition=%wide.region_12.12_spmd, body=%wide.region_10.11_spmd.sunk | while | flops 1022541056 | bytes 79656208 | solution.py:207
  521.2 68.9 %reduce-scatter.14.cloned.1.call-done = bf16[256,640]{0,1:T(8,128)(2,1)} async-done(((bf16[2048,640]{0,1:T(8,128)(2,1)}), bf16[256,640]{0,1:T(8,128)(2,1)}) %reduce-scatter.14.cloned.1.call-update) | async-done | bytes 327696 | tf_op jit(solution)/shard_map/while/body/eval_jaxpr/reduce_scatter | solution.py:215
  606.1 79.8 %while.46 = (s32[]{:T(128)}, f32[5,768,64]{1,2,0:T(8,128)}, bf16[5,2048,64]{1,2,0:T(8,128)(2,1)}, bf16[5,2048,64]{1,2,0:T(8,128)(2,1)}, bf16[5,768,64]{2,1,0:T(8...) while((s32[]{:T(128)}, f32[5,768,64]{1,2,0:T(8,128)}, ...), condition=%wide.region_12.12_spmd, body=%wide.region_10.11_spmd.sunk | while | flops 1022541056 | bytes 79656208 | solution.py:207
  691.8 67.5 %reduce-scatter.14.cloned.1.call-done = bf16[256,640]{0,1:T(8,128)(2,1)} async-done(((bf16[2048,640]{0,1:T(8,128)(2,1)}), bf16[256,640]{0,1:T(8,128)(2,1)}) %reduce-scatter.14.cloned.1.call-update) | async-done | bytes 327696 | tf_op jit(solution)/shard_map/while/body/eval_jaxpr/reduce_scatter | solution.py:215
  779.7 9.3 concatenate.38
  789.1 40.0 %reduce-scatter.12.cloned.1.call-done = bf16[240,3840]{1,0:T(8,128)(2,1)} async-done(((bf16[960,3840]{1,0:T(8,128)(2,1)}), bf16[240,3840]{1,0:T(8,128)(2,1)}) %reduce-scatter.12.cloned.1.call-update) | async-done | bytes 1843216 | tf_op jit(solution)/shard_map/reduce_scatter | solution.py:278
  841.4 21.5 %all-reduce.4 = (bf16[240]{0:T(256)(128)(2,1)S(1)}, bf16[240]{0:T(256)(128)(2,1)S(1)}) all-reduce(bf16[240]{0:T(256)(128)(2,1)S(1)} %dynamic-slice.3, bf16[240]{0:T(256)(128)(2,1)S(1)} %dynamic-slice.5), channel_id=1, replica_groups=mesh['fsdp'=4,'ctx'=4,'tp'=2] {'ctx','tp'}, use_global_device_ids=true, to_apply=%region_17.18 | all-reduce | flops 480 | bytes 1920 | tf_op jit(solution)/shard_map/psum | solution.py:270
  864.1 16.8 %reduce-scatter.10.cloned.1.call-done = bf16[240,2560]{1,0:T(8,128)(2,1)} async-done(((bf16[960,2560]{1,0:T(8,128)(2,1)}), bf16[240,2560]{1,0:T(8,128)(2,1)}) %reduce-scatter.10.cloned.1.call-update) | async-done | bytes 1228816 | tf_op jit(solution)/shard_map/reduce_scatter | solution.py:275
  884.3 77.4 %all-reduce.12.cloned.1.call-done = bf16[240,3840]{1,0:T(8,128)(2,1)} async-done(((bf16[240,3840]{1,0:T(8,128)(2,1)}), bf16[240,3840]{1,0:T(8,128)(2,1)}) %all-reduce.12.cloned.1.call-update) | async-done | bytes 1843216 | tf_op jit(solution)/shard_map/psum | solution.py:273
  965.0 80.2 %all-reduce.10.cloned.1.call-done = bf16[240,2560]{1,0:T(8,128)(2,1)} async-done(((bf16[240,2560]{1,0:T(8,128)(2,1)}), bf16[240,2560]{1,0:T(8,128)(2,1)}) %all-reduce.10.cloned.1.call-update) | async-done | bytes 1228816 | tf_op jit(solution)/shard_map/psum | solution.py:269
  (457 shorter events, 400.5 us)
Async XLA Ops:
  7.2 22.9 %copy-start.11 = (bf16[2,256,960]{1,2,0:T(8,128)(2,1)S(1)}, bf16[2,256,960]{1,2,0:T(8,128)(2,1)}, u32[]{:S(2)}) copy-start(bf16[2,256,960]{1,2,0:T(8,128)(2,1)} %param.16) | copy-start | bytes 2949124
  7.2 22.9 %all-gather.12.cloned.1.call-start = ((), (), s32[]{:S(2)}) async-start(), calls=%async_computation.6 | async-start | bytes 1536000 | tf_op jit(solution)/shard_map/all_gather | solution.py:125
  7.9 45.6 %all-gather.10.cloned.1.call-start = ((), (), s32[]{:S(2)}) async-start(), calls=%async_computation.5 | async-start | bytes 2457600 | tf_op jit(solution)/shard_map/all_gather | solution.py:124
  8.7 133.9 %all-gather.14.cloned.1.call-start = ((), (), s32[]{:S(2)}) async-start(), calls=%async_computation.7 | async-start | bytes 5898240 | tf_op jit(solution)/shard_map/all_gather | solution.py:142
  20.8 32.8 %copy-start.28 = (f32[960]{0:T(1024)}, f32[960]{0:T(1024)S(1)}, u32[]{:S(2)}) copy-start(f32[960]{0:T(1024)S(1)} %convert_element_type.123) | copy-start | bytes 11524
  22.2 31.3 %copy-start.31 = (f32[2,256]{1,0:T(2,128)}, f32[2,256]{1,0:T(2,128)S(1)}, u32[]{:S(2)}) copy-start(f32[2,256]{1,0:T(2,128)S(1)} %add_rsqrt_fusion.1) | copy-start | bytes 6148
  23.0 33.4 %copy-start.21 = (f32[256,32]{0,1:T(8,128)}, f32[256,32]{0,1:T(8,128)S(1)}, u32[]{:S(2)}) copy-start(f32[256,32]{0,1:T(8,128)S(1)} %get-tuple-element.374) | copy-start | bytes 98308
  34.4 208.9 %all-gather.16.cloned.1.call-start = ((), (), s32[]{:S(2)}) async-start(), calls=%async_computation.8 | async-start | bytes 2457600 | tf_op jit(solution)/shard_map/all_gather | solution.py:126
  35.0 213.7 %all-gather.26.cloned.1.call-start = ((), (), s32[]{:S(2)}) async-start(), calls=%async_computation.14 | async-start | bytes 2949120 | tf_op jit(solution)/shard_map/all_gather | solution.py:168
  35.6 213.1 %all-gather.24.cloned.1.call-start = ((), (), s32[]{:S(2)}) async-start(), calls=%async_computation.12 | async-start | bytes 3072000 | tf_op jit(solution)/shard_map/all_gather | solution.py:160
  36.2 220.1 %all-gather.22.cloned.1.call-start = ((), (), s32[]{:S(2)}) async-start(), calls=%async_computation.11 | async-start | bytes 3072000 | tf_op jit(solution)/shard_map/all_gather | solution.py:159
  36.9 246.2 %all-gather.18.cloned.1.call-start = ((), (), s32[]{:S(2)}) async-start(), calls=%async_computation.9 | async-start | bytes 2949120 | tf_op jit(solution)/shard_map/all_gather | solution.py:167
  247.7 61.7 %all-gather.20.cloned.1.call-start = ((), (), s32[]{:S(2)}) async-start(), calls=%async_computation.10 | async-start | bytes 3072000 | tf_op jit(solution)/shard_map/all_gather | solution.py:158
  248.5 133.4 %reduce-scatter.8.cloned.1.call-start = ((), (), s32[]{:S(2)}) async-start(), calls=%async_computation.15 | async-start | bytes 5898240 | tf_op jit(solution)/shard_map/reduce_scatter | solution.py:193
  329.7 84.9 %reduce-scatter.6.cloned.1.call-start = ((), (), s32[]{:S(2)}) async-start(), calls=%async_computation.13 | async-start | bytes 2949120 | tf_op jit(solution)/shard_map/reduce_scatter | solution.py:176
  352.2 62.4 %copy-start.10 = (bf16[2,256,960]{1,2,0:T(8,128)(2,1)S(1)}, bf16[2,256,960]{1,2,0:T(8,128)(2,1)}, u32[]{:S(2)}) copy-start(bf16[2,256,960]{1,2,0:T(8,128)(2,1)} %param.17) | copy-start | bytes 2949124
  421.6 168.5 %reduce-scatter.14.cloned.1.call-start = ((), (), s32[]{:S(2)}) async-start(), calls=%async_computation.20 | async-start | bytes 2949120 | tf_op jit(solution)/shard_map/while/body/eval_jaxpr/reduce_scatter | solution.py:215
  519.0 71.1 %copy-start.13 = (f32[2,256,640]{1,2,0:T(8,128)S(1)}, f32[2,256,640]{1,2,0:T(8,128)}, u32[]{:S(2)}) copy-start(f32[2,256,640]{1,2,0:T(8,128)} %get-tuple-element.691) | copy-start | bytes 3932164 | tf_op jit(solution)/shard_map/while
  592.2 167.1 %reduce-scatter.14.cloned.1.call-start = ((), (), s32[]{:S(2)}) async-start(), calls=%async_computation.20 | async-start | bytes 2949120 | tf_op jit(solution)/shard_map/while/body/eval_jaxpr/reduce_scatter | solution.py:215
  689.5 69.8 %copy-start.13 = (f32[2,256,640]{1,2,0:T(8,128)S(1)}, f32[2,256,640]{1,2,0:T(8,128)}, u32[]{:S(2)}) copy-start(f32[2,256,640]{1,2,0:T(8,128)} %get-tuple-element.691) | copy-start | bytes 3932164 | tf_op jit(solution)/shard_map/while
  761.4 67.7 %reduce-scatter.12.cloned.1.call-start = ((), (), s32[]{:S(2)}) async-start(), calls=%async_computation.18 | async-start | bytes 9216000 | tf_op jit(solution)/shard_map/reduce_scatter | solution.py:278
  761.9 119.0 %reduce-scatter.10.cloned.1.call-start = ((), (), s32[]{:S(2)}) async-start(), calls=%async_computation.16 | async-start | bytes 6144000 | tf_op jit(solution)/shard_map/reduce_scatter | solution.py:275
  789.0 172.6 %all-reduce.12.cloned.1.call-start = ((), (), s32[]{:S(2)}) async-start(), calls=%async_computation.19 | async-start | bytes 3686400 | tf_op jit(solution)/shard_map/psum | solution.py:273
  829.1 216.1 %all-reduce.10.cloned.1.call-start = ((), (), s32[]{:S(2)}) async-start(), calls=%async_computation.17 | async-start | bytes 2457600 | tf_op jit(solution)/shard_map/psum | solution.py:269
  (83 other events, 196.6 us)
Sparse Core Ops, SparseCore 0:
  9.6 20.4 all-gather.11
  31.6 21.8 all-gather.9
  56.3 86.2 all-gather.13
  144.0 20.0 all-gather.15
  165.4 31.5 all-gather.25
  198.5 24.6 all-gather.23
  224.8 24.5 all-gather.21
  251.5 31.5 all-gather.17
  284.7 24.6 all-gather.19
  329.8 51.9 reduce-scatter.7
  384.2 30.3 reduce-scatter.5
  519.1 70.9 reduce-scatter.13
  689.7 69.5 reduce-scatter.13
  764.4 64.6 reduce-scatter.11
  831.7 49.1 reduce-scatter.9
  883.2 78.4 all-reduce.11
  965.0 80.1 all-reduce.9
where the time goes:
time: 1060 us
  waiting for transfers between devices  568 us (54%)
  matrix products  260 us (25%)
  local copies, waits for them, and re-layouts  112 us (11%)
  other arithmetic  60.4 us (6%)
  blocking collectives  35.6 us (3%)
  between operations  16 us (2%)
    reduce_scatter x2, waiting for transfers between devices, attend_back(): lax.psum_scatter(back_keyval.astype(jnp.bfloat16), ('ctx', 'tp'), scatter...  136 us
    all_gather x1, waiting for transfers between devices, on_device(): lax.all_gather(keyval_low, ('ctx', 'tp'), axis=1, tiled=True)  84 us
    psum x1, waiting for transfers between devices, on_device(): lax.psum(attention_term.astype(jnp.bfloat16), ('ctx', 'tp'))  80.2 us
    psum x1, waiting for transfers between devices, on_device(): feed_total = lax.psum(feed_term.astype(jnp.bfloat16), 'ctx')  77.4 us
    dot_general x20, matrix products, masked_scores(): jnp.einsum('qd,kd->qk', query_group, key_group, preferred_element_type=jn...  60.3 us
    reduce_scatter x1, waiting for transfers between devices, on_device(): lax.psum_scatter(feed_total, 'fsdp', scatter_dimension=0, tiled=True)  40 us
    dot_general x10, matrix products, head_forward(): jnp.einsum('qk,kd->qd', weights, value_group, preferred_element_type=jnp....  33.4 us
    reduce_scatter x1, waiting for transfers between devices, on_device(): lax.psum_scatter(branch_part.astype(jnp.bfloat16), 'tp', scatter_dimensio...  30.1 us
  transfers between devices with their start and end apart: 17, of which 13 were waited for; matrix products, arithmetic and copies ran while one was open for 19% of the time, Pallas kernels for 0%

commit v1 on v0

--- a/solution.py
+++ b/solution.py
@@ -11,6 +11,27 @@
 KEY_WIDTH = 320
 EPS = 1e-05
 THETA = 10000.0
+
+
+def ring_gather(array, axis, dim):
+    peers, index, span = (lax.axis_size(axis), lax.axis_index(axis), array.shape[dim])
+    right = [(i, (i + 1) % peers) for i in range(peers)]
+    downward = [(i, (i - 1) % peers) for i in range(peers)]
+    out = jnp.zeros((*array.shape[:dim], peers * span, *array.shape[dim + 1 :]), array.dtype)
+    out = lax.dynamic_update_slice_in_dim(out, array, index * span, axis=dim)
+    from_left = from_right = array
+    middle = peers // 2
+    for step in range(1, middle + 1):
+        from_left = lax.ppermute(from_left, axis, right)
+        out = lax.dynamic_update_slice_in_dim(
+            out, from_left, (index - step) % peers * span, axis=dim
+        )
+        if step < peers - middle:
+            from_right = lax.ppermute(from_right, axis, downward)
+            out = lax.dynamic_update_slice_in_dim(
+                out, from_right, (index + step) % peers * span, axis=dim
+            )
+    return out
 
 
 def rope_tables(token_positions, first_place):
@@ -139,7 +160,7 @@
         ],
         -1,
     ).astype(jnp.bfloat16)
-    keyval_gathered = lax.all_gather(keyval_low, ("ctx", "tp"), axis=1, tiled=True)
+    keyval_gathered = ring_gather(keyval_low, ("ctx", "tp"), 1)
     query_heads = to_heads(query_low, sequence_count, token_positions)
     stacked = (
         keyval_gathered.reshape(sequence_count, SEQUENCE_LENGTH, 2, KEYVAL_HEADS, HEAD_WIDTH)

time: 1060 us -> 1070 us (level)
  starting transfers between devices: 1.31 us -> 16.1 us
  waiting for transfers between devices: 568 us -> 554 us
    ppermute x0 -> x7, waiting for transfers between devices: none -> 91 us  [the longest x4 88.3 us: ring_gather(): from_left = lax.ppermute(from_left, axis, right)]
    all_gather x1 -> x0, waiting for transfers between devices: 84 us -> none  [on_device(): lax.all_gather(keyval_low, ('ctx', 'tp'), axis=1, tiled=True)]
    all_gather x1, waiting for transfers between devices: 16 us -> 0.01 us  [on_device(): lax.all_gather(w_query, 'fsdp', axis=0, tiled=True)]
    ppermute x0 -> x7, starting transfers between devices: none -> 15.3 us  [the longest x4 9.22 us: ring_gather(): from_left = lax.ppermute(from_left, axis, right)]
  transfers between devices with their start and end apart: 17 -> 23, of which waited for: 13 -> 16; matrix products, arithmetic and copies ran while one was open for 19% -> 19% of each run, Pallas kernels for 0% -> 0%
where the time goes in v1:
time: 1070 us; the launch traced here: 1060 us
  waiting for transfers between devices  554 us (52%)
  matrix products  260 us (24%)
  local copies, waits for them, and re-layouts  121 us (11%)
  other arithmetic  58.3 us (5%)
  blocking collectives  35.6 us (3%)
  between operations  16.3 us (2%)
  starting transfers between devices  16.1 us (2%)
    reduce_scatter x2, waiting for transfers between devices, attend_back(): lax.psum_scatter(back_keyval.astype(jnp.bfloat16), ('ctx', 'tp'), scatter...  137 us
    ppermute x4, waiting for transfers between devices, ring_gather(): from_left = lax.ppermute(from_left, axis, right)  88.3 us
    psum x1, waiting for transfers between devices, on_device(): lax.psum(attention_term.astype(jnp.bfloat16), ('ctx', 'tp'))  80.3 us
    psum x1, waiting for transfers between devices, on_device(): feed_total = lax.psum(feed_term.astype(jnp.bfloat16), 'ctx')  77.4 us
    dot_general x20, matrix products, masked_scores(): jnp.einsum('qd,kd->qk', query_group, key_group, preferred_element_type=jn...  60.1 us
    reduce_scatter x1, waiting for transfers between devices, on_device(): lax.psum_scatter(feed_total, 'fsdp', scatter_dimension=0, tiled=True)  40.3 us
    dot_general x10, matrix products, head_forward(): jnp.einsum('qk,kd->qd', weights, value_group, preferred_element_type=jnp....  33.4 us
    reduce_scatter x1, waiting for transfers between devices, on_device(): lax.psum_scatter(branch_part.astype(jnp.bfloat16), 'tp', scatter_dimensio...  29.9 us
  transfers between devices with their start and end apart: 23, of which 16 were waited for; matrix products, arithmetic and copies ran while one was open for 19% of the time, Pallas kernels for 0%

profile of v1, /device:TPU:0, one launch (start us, length us, event | category | flops | bytes accessed | tf_op | source)
XLA Modules:
  0.0 1063.4 jit_solution(17360830257828506106)
XLA Ops:
  12.4 8.3 all-reduce.6
  21.9 8.2 all-gather.11.cloned.1.call-done
  38.4 25.2 %collective-permute-done = bf16[2,256,640]{2,1,0:T(8,128)(2,1)} collective-permute-done((bf16[2,256,640]{2,1,0:T(8,128)(2,1)S(1)}, bf16[2,256,640]{2,1,0:T(8,128)(2,1)}, u32[]{:S(2)}, u32[]{:S(2)}) %collective-permute-start) | collective-permute-done | bytes 655392 | tf_op jit(solution)/shard_map/ppermute | solution.py:25
  69.5 34.2 %collective-permute-done.2 = bf16[2,256,640]{2,1,0:T(8,128)(2,1)S(1)} collective-permute-done((bf16[2,256,640]{2,1,0:T(8,128)(2,1)}, bf16[2,256,640]{2,1,0:T(8,128)(2,1)S(1)}, u32[]{:S(2)}, u32[]{:S(2)}) %collective-permute-start.2) | collective-permute-done | bytes 655392 | tf_op jit(solution)/shard_map/ppermute | solution.py:25
  120.2 22.9 %collective-permute-done.4 = bf16[2,256,640]{2,1,0:T(8,128)(2,1)} collective-permute-done((bf16[2,256,640]{2,1,0:T(8,128)(2,1)S(1)}, bf16[2,256,640]{2,1,0:T(8,128)(2,1)}, u32[]{:S(2)}, u32[]{:S(2)}) %collective-permute-start.4) | collective-permute-done | bytes 655392 | tf_op jit(solution)/shard_map/ppermute | solution.py:25
  171.7 80.4 %while.43 = (s32[]{:T(128)}, bf16[10,768,64]{1,2,0:T(8,128)(2,1)S(1)}, f32[10,768]{1,0:T(8,128)S(1)}, f32[10,768]{1,0:T(8,128)S(1)}, bf16[10,768,64]{2,1,0:T(8,1...) while((s32[]{:T(128)}, ...), condition=%wide.region_4.5_spmd.clone, body=%wide.region_1.4_spmd.clone.sunk | while | flops 426244608 | bytes 19846260 | solution.py:172
  262.4 7.5 fusion.58
  270.0 20.7 %all-gather.15.cloned.1.call-done = bf16[2,512,960]{1,2,0:T(8,128)(2,1)} async-done(((bf16[2,256,960]{1,2,0:T(8,128)(2,1)}), bf16[2,512,960]{1,2,0:T(8,128)(2,1)}) %all-gather.15.cloned.1.call-update) | async-done | bytes 1966096 | tf_op jit(solution)/shard_map/all_gather | solution.py:188
  290.7 7.6 fusion.64
  298.3 18.6 %all-gather.17.cloned.1.call-done = bf16[960,1280]{1,0:T(8,128)(2,1)} async-done(((bf16[240,1280]{1,0:T(8,128)(2,1)}), bf16[960,1280]{1,0:T(8,128)(2,1)}) %all-gather.17.cloned.1.call-update) | async-done | bytes 2457616 | tf_op jit(solution)/shard_map/all_gather | solution.py:179
  316.9 11.9 %multiply_convert_fusion.2 = (bf16[2,512,1280]{2,1,0:T(8,128)(2,1)S(1)}, bf16[2,512,1280]{2,1,0:T(8,128)(2,1)S(1)}, bf16[2,512,1280]{2,1,0:T(8,128)(2,1)}) fusion(f32[2,512,1280]{2,1,0:T(8,128)} %fusion.58, f32[2,512,1280]{2,1,0:T(8,128)} %fusion.64, bf16[2,512,960]{1,2,0:T(8,128)(2,1)} %all-gather.15.cloned.1.call-done, ...), kind=kOutput, calls=%fused_computation.71 | convolution fusion | flops 2536243200 | bytes 22773760 | tf_op jit(solution)/shard_map/dot_general | solution.py:191
  359.9 29.6 %reduce-scatter.8.cloned.1.call-done = f32[2,256,960]{1,2,0:T(8,128)} async-done(((f32[2,512,960]{1,2,0:T(8,128)}), f32[2,256,960]{1,2,0:T(8,128)}) %reduce-scatter.8.cloned.1.call-update) | async-done | bytes 1966096 | tf_op jit(solution)/shard_map/reduce_scatter | solution.py:214
  392.3 29.9 %reduce-scatter.6.cloned.1.call-done = bf16[2,256,960]{1,2,0:T(8,128)(2,1)} async-done(((bf16[2,512,960]{1,2,0:T(8,128)(2,1)}), bf16[2,256,960]{1,2,0:T(8,128)(2,1)}) %reduce-scatter.6.cloned.1.call-update) | async-done | bytes 983056 | tf_op jit(solution)/shard_map/reduce_scatter | solution.py:197
  428.7 340.2 %while.45 = (s32[]{:T(128)}, f32[2,5,768,64]{2,3,1,0:T(8,128)}, f32[2,256,640]{1,2,0:T(8,128)}, bf16[2,5,768,64]{3,2,1,0:T(8,128)(2,1)}, bf16[2,5,2048,64]{2,3,1...) while((s32[]{:T(128)}, f32[2,5,768,64]{2,3,1,0:T(8,128)}, ...), condition=%wide.region_14.15_spmd.clone, body=%wide.region_9.14_spmd.clone.sunk | while | flops 1025588480 | bytes 125203080 | solution.py:254
  442.9 79.9 %while.46 = (s32[]{:T(128)}, f32[5,768,64]{1,2,0:T(8,128)}, bf16[5,2048,64]{1,2,0:T(8,128)(2,1)}, bf16[5,2048,64]{1,2,0:T(8,128)(2,1)}, bf16[5,768,64]{2,1,0:T(8...) while((s32[]{:T(128)}, f32[5,768,64]{1,2,0:T(8,128)}, ...), condition=%wide.region_12.12_spmd, body=%wide.region_10.11_spmd.sunk | while | flops 1022541056 | bytes 79656208 | solution.py:228
  528.5 68.9 %reduce-scatter.14.cloned.1.call-done = bf16[256,640]{0,1:T(8,128)(2,1)} async-done(((bf16[2048,640]{0,1:T(8,128)(2,1)}), bf16[256,640]{0,1:T(8,128)(2,1)}) %reduce-scatter.14.cloned.1.call-update) | async-done | bytes 327696 | tf_op jit(solution)/shard_map/while/body/eval_jaxpr/reduce_scatter | solution.py:236
  613.4 79.9 %while.46 = (s32[]{:T(128)}, f32[5,768,64]{1,2,0:T(8,128)}, bf16[5,2048,64]{1,2,0:T(8,128)(2,1)}, bf16[5,2048,64]{1,2,0:T(8,128)(2,1)}, bf16[5,768,64]{2,1,0:T(8...) while((s32[]{:T(128)}, f32[5,768,64]{1,2,0:T(8,128)}, ...), condition=%wide.region_12.12_spmd, body=%wide.region_10.11_spmd.sunk | while | flops 1022541056 | bytes 79656208 | solution.py:228
  699.1 67.7 %reduce-scatter.14.cloned.1.call-done = bf16[256,640]{0,1:T(8,128)(2,1)} async-done(((bf16[2048,640]{0,1:T(8,128)(2,1)}), bf16[256,640]{0,1:T(8,128)(2,1)}) %reduce-scatter.14.cloned.1.call-update) | async-done | bytes 327696 | tf_op jit(solution)/shard_map/while/body/eval_jaxpr/reduce_scatter | solution.py:236
  787.2 9.3 concatenate.38
  796.6 40.3 %reduce-scatter.12.cloned.1.call-done = bf16[240,3840]{1,0:T(8,128)(2,1)} async-done(((bf16[960,3840]{1,0:T(8,128)(2,1)}), bf16[240,3840]{1,0:T(8,128)(2,1)}) %reduce-scatter.12.cloned.1.call-update) | async-done | bytes 1843216 | tf_op jit(solution)/shard_map/reduce_scatter | solution.py:299
  849.2 21.5 %all-reduce.4 = (bf16[240]{0:T(256)(128)(2,1)S(1)}, bf16[240]{0:T(256)(128)(2,1)S(1)}) all-reduce(bf16[240]{0:T(256)(128)(2,1)S(1)} %dynamic-slice.3, bf16[240]{0:T(256)(128)(2,1)S(1)} %dynamic-slice.5), channel_id=1, replica_groups=mesh['fsdp'=4,'ctx'=4,'tp'=2] {'ctx','tp'}, use_global_device_ids=true, to_apply=%region_17.18 | all-reduce | flops 480 | bytes 1920 | tf_op jit(solution)/shard_map/psum | solution.py:291
  871.9 16.8 %reduce-scatter.10.cloned.1.call-done = bf16[240,2560]{1,0:T(8,128)(2,1)} async-done(((bf16[960,2560]{1,0:T(8,128)(2,1)}), bf16[240,2560]{1,0:T(8,128)(2,1)}) %reduce-scatter.10.cloned.1.call-update) | async-done | bytes 1228816 | tf_op jit(solution)/shard_map/reduce_scatter | solution.py:296
  892.1 77.4 %all-reduce.12.cloned.1.call-done = bf16[240,3840]{1,0:T(8,128)(2,1)} async-done(((bf16[240,3840]{1,0:T(8,128)(2,1)}), bf16[240,3840]{1,0:T(8,128)(2,1)}) %all-reduce.12.cloned.1.call-update) | async-done | bytes 1843216 | tf_op jit(solution)/shard_map/psum | solution.py:294
  972.8 80.3 %all-reduce.10.cloned.1.call-done = bf16[240,2560]{1,0:T(8,128)(2,1)} async-done(((bf16[240,2560]{1,0:T(8,128)(2,1)}), bf16[240,2560]{1,0:T(8,128)(2,1)}) %all-reduce.10.cloned.1.call-update) | async-done | bytes 1228816 | tf_op jit(solution)/shard_map/psum | solution.py:290
  (494 shorter events, 439.0 us)
Async XLA Ops:
  7.2 22.9 %all-gather.11.cloned.1.call-start = ((), (), s32[]{:S(2)}) async-start(), calls=%async_computation.6 | async-start | bytes 1536000 | tf_op jit(solution)/shard_map/all_gather | solution.py:146
  8.0 106.6 %all-gather.9.cloned.1.call-start = ((), (), s32[]{:S(2)}) async-start(), calls=%async_computation.5 | async-start | bytes 2457600 | tf_op jit(solution)/shard_map/all_gather | solution.py:145
  8.7 248.3 %all-gather.13.cloned.1.call-start = ((), (), s32[]{:S(2)}) async-start(), calls=%async_computation.7 | async-start | bytes 2457600 | tf_op jit(solution)/shard_map/all_gather | solution.py:147
  9.4 253.0 %all-gather.23.cloned.1.call-start = ((), (), s32[]{:S(2)}) async-start(), calls=%async_computation.13 | async-start | bytes 2949120 | tf_op jit(solution)/shard_map/all_gather | solution.py:189
  10.0 252.4 %all-gather.21.cloned.1.call-start = ((), (), s32[]{:S(2)}) async-start(), calls=%async_computation.11 | async-start | bytes 3072000 | tf_op jit(solution)/shard_map/all_gather | solution.py:181
  10.6 259.4 %all-gather.19.cloned.1.call-start = ((), (), s32[]{:S(2)}) async-start(), calls=%async_computation.10 | async-start | bytes 3072000 | tf_op jit(solution)/shard_map/all_gather | solution.py:180
  21.9 124.0 %copy-start.21 = (f32[256,32]{0,1:T(8,128)}, f32[256,32]{0,1:T(8,128)S(1)}, u32[]{:S(2)}) copy-start(f32[256,32]{0,1:T(8,128)S(1)} %get-tuple-element.374) | copy-start | bytes 98308
  33.6 30.0 %collective-permute-start = (bf16[2,256,640]{2,1,0:T(8,128)(2,1)S(1)}, bf16[2,256,640]{2,1,0:T(8,128)(2,1)}, u32[]{:S(2)}, u32[]{:S(2)}) collective-permute-start(bf16[2,256,640]{2,1,0:T(8,128)(2,1)S(1)} %pad_maximum_fusion.4), channel_id=1, source_target_pairs={{0,1},{1,2},{2,3},{3,4},{4,5},{5,6},{6,7},{7,0},{8,9},{9,10},{10,1... | collective-permute-start | bytes 1966088 | tf_op jit(solution)/shard_map/ppermute | solution.py:25
  35.1 31.6 %collective-permute-start.1 = (bf16[2,256,640]{2,1,0:T(8,128)(2,1)S(1)}, bf16[2,256,640]{2,1,0:T(8,128)(2,1)}, u32[]{:S(2)}, u32[]{:S(2)}) collective-permute-start(bf16[2,256,640]{2,1,0:T(8,128)(2,1)S(1)} %pad_maximum_fusion.4), channel_id=1, source_target_pairs={{0,7},{1,0},{2,1},{3,2},{4,3},{5,4},{6,5},{7,6},{8,15},{9,8},{10,9... | collective-permute-start | bytes 1966088 | tf_op jit(solution)/shard_map/ppermute | solution.py:30
  63.6 40.1 %collective-permute-start.2 = (bf16[2,256,640]{2,1,0:T(8,128)(2,1)}, bf16[2,256,640]{2,1,0:T(8,128)(2,1)S(1)}, u32[]{:S(2)}, u32[]{:S(2)}) collective-permute-start(bf16[2,256,640]{2,1,0:T(8,128)(2,1)} %collective-permute-done), channel_id=1, source_target_pairs={{0,1},{1,2},{2,3},{3,4},{4,5},{5,6},{6,7},{7,0},{8,9},{9,10},{10,1... | collective-permute-start | bytes 1966088 | tf_op jit(solution)/shard_map/ppermute | solution.py:25
  66.2 224.5 %all-gather.15.cloned.1.call-start = ((), (), s32[]{:S(2)}) async-start(), calls=%async_computation.8 | async-start | bytes 2949120 | tf_op jit(solution)/shard_map/all_gather | solution.py:188
  66.7 53.5 %collective-permute-start.3 = (bf16[2,256,640]{2,1,0:T(8,128)(2,1)}, bf16[2,256,640]{2,1,0:T(8,128)(2,1)}, u32[]{:S(2)}, u32[]{:S(2)}) collective-permute-start(bf16[2,256,640]{2,1,0:T(8,128)(2,1)} %collective-permute-done.1), channel_id=1, source_target_pairs={{0,7},{1,0},{2,1},{3,2},{4,3},{5,4},{6,5},{7,6},{8,15},{9,8},{10,9... | collective-permute-start | bytes 1966088 | tf_op jit(solution)/shard_map/ppermute | solution.py:30
  103.7 39.5 %collective-permute-start.4 = (bf16[2,256,640]{2,1,0:T(8,128)(2,1)S(1)}, bf16[2,256,640]{2,1,0:T(8,128)(2,1)}, u32[]{:S(2)}, u32[]{:S(2)}) collective-permute-start(bf16[2,256,640]{2,1,0:T(8,128)(2,1)S(1)} %collective-permute-done.2), channel_id=1, source_target_pairs={{0,1},{1,2},{2,3},{3,4},{4,5},{5,6},{6,7},{7,0},{8,9},{9,10},{10,1... | collective-permute-start | bytes 1966088 | tf_op jit(solution)/shard_map/ppermute | solution.py:25
  120.2 32.7 %collective-permute-start.5 = (bf16[2,256,640]{2,1,0:T(8,128)(2,1)}, bf16[2,256,640]{2,1,0:T(8,128)(2,1)}, u32[]{:S(2)}, u32[]{:S(2)}) collective-permute-start(bf16[2,256,640]{2,1,0:T(8,128)(2,1)} %collective-permute-done.3), channel_id=1, source_target_pairs={{0,7},{1,0},{2,1},{3,2},{4,3},{5,4},{6,5},{7,6},{8,15},{9,8},{10,9... | collective-permute-start | bytes 1966088 | tf_op jit(solution)/shard_map/ppermute | solution.py:30
  143.1 19.0 %collective-permute-start.6 = (bf16[2,256,640]{2,1,0:T(8,128)(2,1)}, bf16[2,256,640]{2,1,0:T(8,128)(2,1)}, u32[]{:S(2)}, u32[]{:S(2)}) collective-permute-start(bf16[2,256,640]{2,1,0:T(8,128)(2,1)} %collective-permute-done.4), channel_id=1, source_target_pairs={{0,1},{1,2},{2,3},{3,4},{4,5},{5,6},{6,7},{7,0},{8,9},{9,10},{10,1... | collective-permute-start | bytes 1966088 | tf_op jit(solution)/shard_map/ppermute | solution.py:25
  261.4 55.5 %all-gather.17.cloned.1.call-start = ((), (), s32[]{:S(2)}) async-start(), calls=%async_computation.9 | async-start | bytes 3072000 | tf_op jit(solution)/shard_map/all_gather | solution.py:179
  262.1 127.4 %reduce-scatter.8.cloned.1.call-start = ((), (), s32[]{:S(2)}) async-start(), calls=%async_computation.14 | async-start | bytes 5898240 | tf_op jit(solution)/shard_map/reduce_scatter | solution.py:214
  337.4 84.7 %reduce-scatter.6.cloned.1.call-start = ((), (), s32[]{:S(2)}) async-start(), calls=%async_computation.12 | async-start | bytes 2949120 | tf_op jit(solution)/shard_map/reduce_scatter | solution.py:197
  428.9 168.5 %reduce-scatter.14.cloned.1.call-start = ((), (), s32[]{:S(2)}) async-start(), calls=%async_computation.19 | async-start | bytes 2949120 | tf_op jit(solution)/shard_map/while/body/eval_jaxpr/reduce_scatter | solution.py:236
  599.5 167.3 %reduce-scatter.14.cloned.1.call-start = ((), (), s32[]{:S(2)}) async-start(), calls=%async_computation.19 | async-start | bytes 2949120 | tf_op jit(solution)/shard_map/while/body/eval_jaxpr/reduce_scatter | solution.py:236
  768.9 68.0 %reduce-scatter.12.cloned.1.call-start = ((), (), s32[]{:S(2)}) async-start(), calls=%async_computation.17 | async-start | bytes 9216000 | tf_op jit(solution)/shard_map/reduce_scatter | solution.py:299
  769.6 119.2 %reduce-scatter.10.cloned.1.call-start = ((), (), s32[]{:S(2)}) async-start(), calls=%async_computation.15 | async-start | bytes 6144000 | tf_op jit(solution)/shard_map/reduce_scatter | solution.py:296
  796.5 172.9 %all-reduce.12.cloned.1.call-start = ((), (), s32[]{:S(2)}) async-start(), calls=%async_computation.18 | async-start | bytes 3686400 | tf_op jit(solution)/shard_map/psum | solution.py:294
  836.9 216.1 %all-reduce.10.cloned.1.call-start = ((), (), s32[]{:S(2)}) async-start(), calls=%async_computation.16 | async-start | bytes 2457600 | tf_op jit(solution)/shard_map/psum | solution.py:290
  (94 other events, 622.1 us)
Sparse Core Ops, SparseCore 0:
  9.6 20.4 all-gather.10
  31.6 21.8 all-gather.8
  55.1 21.8 all-gather.12
  78.4 65.1 all-gather.22
  145.0 23.8 all-gather.20
  170.3 24.6 all-gather.18
  261.5 29.1 all-gather.14
  292.2 24.6 all-gather.16
  337.5 51.9 reduce-scatter.7
  391.7 30.3 reduce-scatter.5
  526.4 70.9 reduce-scatter.13
  697.0 69.7 reduce-scatter.13
  772.2 64.6 reduce-scatter.11
  839.5 49.1 reduce-scatter.9
  891.0 78.4 all-reduce.11
  972.9 80.1 all-reduce.9
